TPU v7x, 32 devices: a whole 2x2x4 slice. The times are simulated.
32 devices in a mesh: seq: 8 (over z, x), fsdp: 4 (over y, core).
Axes of the slice: x: 2, y: 2, z: 4, core: 2. Of those that a mesh axis runs over, the one named last changes fastest.
Arguments:
- inputs: bfloat16 [4, 2048, 1536], P(None, ('seq', 'fsdp')), may hold values from -6 to 6
- cotangent: bfloat16 [4, 2048, 1536], P(None, ('seq', 'fsdp')), may hold values from -6 to 6
- dilated_kernel_weight: bfloat16 [1536, 3, 768], P('seq', None, 'fsdp'), may hold values from -0.09375 to 0.09375
- point_weight: bfloat16 [1536, 768], P('seq', 'fsdp'), may hold values from -0.21875 to 0.21875
Outputs:
- outputs: bfloat16 [4, 2048, 1536], P(None, ('seq', 'fsdp'))
- grad_inputs: bfloat16 [4, 2048, 1536], P(None, ('seq', 'fsdp'))
- grad_conv: float32 [1536, 3, 768], P('seq', None, 'fsdp')
- grad_point: float32 [1536, 768], P('seq', 'fsdp')
All inputs are finite; a program needn't handle non-finite values.
Results may differ from a plain program's by a relative error of at most 0.0053.
Values may be sent and summed in bfloat16 or wider, within the bound.
A program may use at most 128 MiB of HBM per device.

v0:
```python
import math

import jax
import jax.numpy as jnp
from jax import lax
from jax.sharding import PartitionSpec as P


def shifted(x, axis, by):
    peers = lax.axis_size(axis)
    pairs = [(i, i + by) for i in range(peers) if 0 <= i + by < peers]
    return lax.ppermute(x, axis, pairs)


def gelu_value(v):
    return 0.5 * v * (1.0 + lax.erf(v * (1.0 / math.sqrt(2.0))))


def gelu_slope(v):
    return 0.5 * (1.0 + lax.erf(v * (1.0 / math.sqrt(2.0)))) + v * jnp.exp(-0.5 * v * v) * (
        1.0 / math.sqrt(2.0 * math.pi)
    )


def contract_rows(left, right):
    return lax.dot_general(
        left, right, (((0,), (0,)), ((), ())), preferred_element_type=jnp.float32
    )


def body(inputs, cotangent, dilated_kernel_weight, point_weight):
    seqs, bins, kernel_width = inputs.shape
    rows_all = seqs * bins * lax.axis_size("seq") * lax.axis_size("fsdp")
    norm_factor = 1.0 / math.sqrt(rows_all)
    part_conv, part_point = (
        lax.all_gather(dilated_kernel_weight, "seq", axis=0, tiled=True),
        lax.all_gather(point_weight, "seq", axis=0, tiled=True),
    )
    full_conv, full_point = (
        lax.all_gather(part_conv, "fsdp", axis=2, tiled=True),
        lax.all_gather(part_point, "fsdp", axis=1, tiled=True),
    )
    half_kernel_span = full_point.shape[1]
    x = inputs.astype(jnp.float32)
    scale = lax.rsqrt(jnp.mean(x * x, axis=-1, keepdims=True) + 1e-06)
    normed = x * scale
    input_activations = gelu_value(normed).astype(jnp.bfloat16)
    flat_acts = input_activations.reshape(-1, kernel_width)
    acts_back = shifted(input_activations, ("seq", "fsdp"), 2)
    acts_ahead = shifted(input_activations, ("seq", "fsdp"), -2)
    hidden_state = jnp.dot(flat_acts, full_conv[:, 1, :], preferred_element_type=jnp.float32)
    hidden_state = hidden_state + jnp.dot(
        acts_back.reshape(-1, kernel_width), full_conv[:, 0, :], preferred_element_type=jnp.float32
    )
    hidden_state = hidden_state + jnp.dot(
        acts_ahead.reshape(-1, kernel_width), full_conv[:, 2, :], preferred_element_type=jnp.float32
    )
    mid = gelu_value(hidden_state).astype(jnp.bfloat16)
    mixed = lax.dot_general(
        mid, full_point, (((1,), (1,)), ((), ())), preferred_element_type=jnp.float32
    )
    outputs = (
        (x.reshape(-1, kernel_width) + mixed).astype(jnp.bfloat16).reshape(seqs, bins, kernel_width)
    )
    flat_cot = cotangent.reshape(-1, kernel_width)
    back_mid = jnp.dot(flat_cot, full_point, preferred_element_type=jnp.float32)
    hidden_state_gradient = (
        (back_mid * gelu_slope(hidden_state))
        .astype(jnp.bfloat16)
        .reshape(seqs, bins, half_kernel_span)
    )
    grad_later = shifted(hidden_state_gradient, ("seq", "fsdp"), -2)
    grad_earlier = shifted(hidden_state_gradient, ("seq", "fsdp"), 2)
    stacked_tap_inputs = jnp.concatenate(
        [grad_later, hidden_state_gradient, grad_earlier], axis=-1
    ).reshape(-1, 3 * half_kernel_span)
    grad_acts = lax.dot_general(
        stacked_tap_inputs,
        full_conv.reshape(kernel_width, 3 * half_kernel_span),
        (((1,), (1,)), ((), ())),
        preferred_element_type=jnp.float32,
    )
    grad_normed = grad_acts.reshape(seqs, bins, kernel_width) * gelu_slope(normed)
    inner = jnp.mean(grad_normed * x, axis=-1, keepdims=True)
    grad_inputs = (
        cotangent.astype(jnp.float32) + scale * (grad_normed - x * scale * scale * inner)
    ).astype(jnp.bfloat16)
    conv_part = contract_rows(flat_acts, stacked_tap_inputs)
    point_part = contract_rows(flat_cot, mid)
    summed = lax.psum_scatter(
        jnp.concatenate([conv_part, point_part], axis=1).reshape(
            dilated_kernel_weight.shape[0] * lax.axis_size("seq"), 4, half_kernel_span
        ),
        "seq",
        scatter_dimension=0,
        tiled=True,
    )
    reduced = lax.psum_scatter(summed, "fsdp", scatter_dimension=2, tiled=True)
    grad_conv = reduced[:, 0:3, :] * norm_factor
    grad_point = reduced[:, 3, :] * norm_factor
    return (outputs, grad_inputs, grad_conv, grad_point)


def solution(mesh):
    return jax.shard_map(
        body,
        mesh=mesh,
        in_specs=(
            P(None, ("seq", "fsdp"), None),
            P(None, ("seq", "fsdp"), None),
            P("seq", None, "fsdp"),
            P("seq", "fsdp"),
        ),
        out_specs=(
            P(None, ("seq", "fsdp"), None),
            P(None, ("seq", "fsdp"), None),
            P("seq", None, "fsdp"),
            P("seq", "fsdp"),
        ),
        check_vma=False,
    )
```

profile of v0, /device:TPU:0, one launch (start us, length us, event | category | flops | bytes accessed | tf_op | source)
XLA Modules:
  0.0 595.9 jit_solution(8675530676613806458)
XLA Ops:
  7.2 2.0 copy.21
  9.2 64.7 %all-gather.4.cloned.1.call-done = bf16[1536,3,192]{2,1,0:T(4,128)(2,1)} async-done(((bf16[192,3,192]{2,1,0:T(4,128)(2,1)}), bf16[1536,3,192]{2,1,0:T(4,128)(2,1)}) %all-gather.4.cloned.1.call-update) | async-done | bytes 1769488 | tf_op jit(solution)/shard_map/all_gather | solution.py:36
  73.9 5.5 copy.22
  80.3 32.1 %all_gather.14 = bf16[1536,192]{1,0:T(8,128)(2,1)S(1)} all-gather(bf16[192,192]{1,0:T(8,128)(2,1)S(1)} %copy-done.6), channel_id=1, replica_groups=mesh['seq'=8,'fsdp'=4] {'seq'}, dimensions={0}, use_global_device_ids=true | all-gather | bytes 663552 | tf_op jit(solution)/shard_map/all_gather | solution.py:37
  115.6 4.6 collective-permute-start
  120.2 35.3 %all-gather.6.cloned.1.call-done = bf16[1536,3,768]{0,2,1:T(8,128)(2,1)} async-done(((bf16[1536,3,192]{0,2,1:T(8,128)(2,1)}), bf16[1536,3,768]{0,2,1:T(8,128)(2,1)}) %all-gather.6.cloned.1.call-update) | async-done | bytes 7077904 | tf_op jit(solution)/shard_map/all_gather | solution.py:40
  155.4 2.5 fusion.3
  157.9 2.5 fusion.1
  160.4 2.5 fusion.9
  163.0 24.9 %all-gather.8.cloned.1.call-done = bf16[1536,768]{0,1:T(8,128)(2,1)} async-done(((bf16[1536,192]{0,1:T(8,128)(2,1)}), bf16[1536,768]{0,1:T(8,128)(2,1)}) %all-gather.8.cloned.1.call-update) | async-done | bytes 2359312 | tf_op jit(solution)/shard_map/all_gather | solution.py:41
  187.8 2.5 fusion.15
  190.4 2.2 collective-permute-start.3
  194.8 15.0 %collective-permute-done.3 = bf16[4,64,768]{2,1,0:T(8,128)(2,1)S(1)} collective-permute-done((bf16[4,64,768]{2,1,0:T(8,128)(2,1)S(1)}, bf16[4,64,768]{2,1,0:T(8,128)(2,1)S(1)}, u32[]{:S(2)}, u32[]{:S(2)}) %collective-permute-start.3) | collective-permute-done | bytes 393248 | tf_op jit(solution)/shard_map/ppermute | solution.py:12
  209.8 7.1 %convolution_bitcast_fusion = f32[1536,2304]{1,0:T(8,128)} fusion(bf16[4,64,1536]{2,1,0:T(8,128)(2,1)S(1)} %multiply_convert_fusion, bf16[4,64,768]{2,1,0:T(8,128)(2,1)S(1)} %collective-permute-done.3, bf16[4,64,768]{2,1,0:T(8,128)(2,1)S(1)} %bitcast.61, bf16[4,64,768]{2,1,0:T(8,128)(2,1)S(1)} %collective-permute-done.2), kind=kOutput, calls=%fused_computation.2 | convolution fusion | flops 1815478272 | bytes 16121856 | tf_op jit(solution)/shard_map/dot_general | solution.py:26
  216.9 6.6 %pad_maximum_fusion = f32[1536,3072]{1,0:T(8,128)S(1)} fusion(f32[1536,768]{1,0:T(8,128)S(1)} %convolution_bitcast_fusion.1, f32[1536,2304]{1,0:T(8,128)} %convolution_bitcast_fusion), kind=kLoop, calls=%fused_computation.1 | loop fusion | flops 4718592 | bytes 37748736 | tf_op jit(solution)/shard_map/concatenate | solution.py:91
  223.5 7.0 %copy.36 = f32[192,4,8,768]{3,2,0,1:T(8,128)} copy(f32[192,4,8,768]{3,2,1,0:T(8,128)S(1)} %bitcast.48) | data formatting | bytes 37748736 | tf_op jit(solution)/shard_map/reshape | solution.py:91
  230.7 316.2 %reduce-scatter.5.cloned.1.call-done = f32[192,4,768]{2,0,1:T(8,128)} async-done(((f32[1536,4,768]{2,0,1:T(8,128)}), f32[192,4,768]{2,0,1:T(8,128)}) %reduce-scatter.5.cloned.1.call-update) | async-done | bytes 2359312 | tf_op jit(solution)/shard_map/reduce_scatter | solution.py:90
  547.0 3.1 copy.30
  550.0 3.1 reshape.73
  554.5 3.4 fusion
  557.9 5.1 multiply_reduce_fusion
  563.0 1.4 add_convert_fusion
  564.4 21.1 %reduce-scatter.7.cloned.1.call-done = f32[192,768]{1,0:T(8,128)} async-done(((f32[768,768]{1,0:T(8,128)}), f32[192,768]{1,0:T(8,128)}) %reduce-scatter.7.cloned.1.call-update) | async-done | bytes 589840
  585.5 1.6 reshape.74
  (48 shorter events, 10.1 us)
Async XLA Ops:
  7.2 66.8 %all-gather.4.cloned.1.call-start = ((), (), s32[]{:S(2)}) async-start(), calls=%async_computation.2 | async-start | bytes 3538944 | tf_op jit(solution)/shard_map/all_gather | solution.py:36
  9.2 146.2 %all-gather.6.cloned.1.call-start = ((), (), s32[]{:S(2)}) async-start(), calls=%async_computation.3 | async-start | bytes 8847360 | tf_op jit(solution)/shard_map/all_gather | solution.py:40
  79.4 0.9 copy-start.6
  79.5 34.1 %copy-start = (bf16[4,64,1536]{2,1,0:T(8,128)(2,1)S(1)}, bf16[4,64,1536]{2,1,0:T(8,128)(2,1)}, u32[]{:S(2)}) copy-start(bf16[4,64,1536]{2,1,0:T(8,128)(2,1)} %param.4) | copy-start | bytes 2359300
  79.5 108.4 %all-gather.8.cloned.1.call-start = ((), (), s32[]{:S(2)}) async-start(), calls=%async_computation.4 | async-start | bytes 2949120 | tf_op jit(solution)/shard_map/all_gather | solution.py:41
  113.5 433.5 %reduce-scatter.5.cloned.1.call-start = ((), (), s32[]{:S(2)}) async-start(), calls=%async_computation.5 | async-start | bytes 21233664 | tf_op jit(solution)/shard_map/reduce_scatter | solution.py:90
  114.3 43.6 %collective-permute-start.1 = (bf16[4,64,1536]{2,1,0:T(8,128)(2,1)S(1)}, bf16[4,64,1536]{2,1,0:T(8,128)(2,1)S(1)}, u32[]{:S(2)}, u32[]{:S(2)}) collective-permute-start(bf16[4,64,1536]{2,1,0:T(8,128)(2,1)S(1)} %multiply_convert_fusion), channel_id=1, source_target_pairs={{2,0},{3,1},{4,2},{5,3},{6,4},{7,5},{8,6},{9,7},{10,8},{11,9},{12,... | collective-permute-start | bytes 2359304 | tf_op jit(solution)/shard_map/ppermute | solution.py:12
  115.6 44.8 %collective-permute-start = (bf16[4,64,1536]{2,1,0:T(8,128)(2,1)S(1)}, bf16[4,64,1536]{2,1,0:T(8,128)(2,1)S(1)}, u32[]{:S(2)}, u32[]{:S(2)}) collective-permute-start(bf16[4,64,1536]{2,1,0:T(8,128)(2,1)S(1)} %multiply_convert_fusion), channel_id=1, source_target_pairs={{0,2},{1,3},{2,4},{3,5},{4,6},{5,7},{6,8},{7,9},{8,10},{9,11},{10,... | collective-permute-start | bytes 2359304 | tf_op jit(solution)/shard_map/ppermute | solution.py:12
  160.4 27.5 %copy-start.4 = (bf16[4,64,1536]{2,1,0:T(8,128)(2,1)S(1)}, bf16[4,64,1536]{2,1,0:T(8,128)(2,1)}, u32[]{:S(2)}) copy-start(bf16[4,64,1536]{2,1,0:T(8,128)(2,1)} %param.5) | copy-start | bytes 2359300
  163.0 31.0 %copy-start.2 = (f32[256,768]{1,0:T(8,128)}, f32[256,768]{1,0:T(8,128)S(1)}, u32[]{:S(2)}) copy-start(f32[256,768]{1,0:T(8,128)S(1)} %fusion.9) | copy-start | bytes 2359300
  190.4 19.4 %collective-permute-start.3 = (bf16[4,64,768]{2,1,0:T(8,128)(2,1)S(1)}, bf16[4,64,768]{2,1,0:T(8,128)(2,1)S(1)}, u32[]{:S(2)}, u32[]{:S(2)}) collective-permute-start(bf16[4,64,768]{2,1,0:T(8,128)(2,1)S(1)} %bitcast.59), channel_id=1, source_target_pairs={{0,2},{1,3},{2,4},{3,5},{4,6},{5,7},{6,8},{7,9},{8,10},{9,11},{10,... | collective-permute-start | bytes 1179656 | tf_op jit(solution)/shard_map/ppermute | solution.py:12
  192.7 17.2 %collective-permute-start.2 = (bf16[4,64,768]{2,1,0:T(8,128)(2,1)S(1)}, bf16[4,64,768]{2,1,0:T(8,128)(2,1)S(1)}, u32[]{:S(2)}, u32[]{:S(2)}) collective-permute-start(bf16[4,64,768]{2,1,0:T(8,128)(2,1)S(1)} %bitcast.60), channel_id=1, source_target_pairs={{2,0},{3,1},{4,2},{5,3},{6,4},{7,5},{8,6},{9,7},{10,8},{11,9},{12,... | collective-permute-start | bytes 1179656 | tf_op jit(solution)/shard_map/ppermute | solution.py:12
  209.8 7.1 %copy-start.7 = (bf16[4,64,768]{2,1,0:T(8,128)(2,1)}, bf16[4,64,768]{2,1,0:T(8,128)(2,1)S(1)}, u32[]{:S(2)}) copy-start(bf16[4,64,768]{2,1,0:T(8,128)(2,1)S(1)} %collective-permute-done.3) | copy-start | bytes 1179652
  209.8 7.1 %copy-start.9 = (bf16[4,64,768]{2,1,0:T(8,128)(2,1)}, bf16[4,64,768]{2,1,0:T(8,128)(2,1)S(1)}, u32[]{:S(2)}) copy-start(bf16[4,64,768]{2,1,0:T(8,128)(2,1)S(1)} %collective-permute-done.2) | copy-start | bytes 1179652
  230.5 355.0 %reduce-scatter.7.cloned.1.call-start = ((), (), s32[]{:S(2)}) async-start(), calls=%async_computation.6 | async-start | bytes 2949120
  553.1 1.1 copy-start.1
  553.1 1.4 copy-start.3
  554.5 3.4 copy-start.8
  554.5 3.4 copy-start.10
  557.9 5.1 copy-start.5
Sparse Core Ops, SparseCore 0:
  10.8 63.1 all-gather.3
  79.6 75.7 all-gather.5
  157.6 30.2 all-gather.7
  230.6 316.2 reduce-scatter.4
  553.3 32.1 reduce-scatter.6
where the time goes:
time: 597 us; the launch traced here: 596 us
  waiting for transfers between devices  477 us (80%)
  blocking collectives  32.1 us (5%)
  matrix products  26.5 us (4%)
  local copies, waits for them, and re-layouts  26.1 us (4%)
  between operations  14 us (2%)
  other arithmetic  10.2 us (2%)
  starting transfers between devices  9.82 us (2%)
    reduce_scatter x1, waiting for transfers between devices, body(): lax.psum_scatter(jnp.concatenate([conv_part, point_part], axis=1).reshape...  316 us
    all_gather x1, waiting for transfers between devices, body(): lax.all_gather(dilated_kernel_weight, 'seq', axis=0, tiled=True)  64.7 us
    all_gather x1, waiting for transfers between devices, body(): lax.all_gather(part_conv, 'fsdp', axis=2, tiled=True)  35.3 us
    all_gather x1, blocking collectives, body(): lax.all_gather(point_weight, 'seq', axis=0, tiled=True)  32.1 us
    all_gather x1, waiting for transfers between devices, body(): lax.all_gather(part_point, 'fsdp', axis=1, tiled=True)  24.9 us
    unnamed x6, waiting for transfers between devices  21.1 us
    ppermute x4, waiting for transfers between devices, shifted(): return lax.ppermute(x, axis, pairs)  15 us
    unnamed x28, local copies, waits for them, and re-layouts  12.4 us
  transfers between devices with their start and end apart: 9, of which 6 were waited for; matrix products, arithmetic and copies ran while one was open for 3% of the time, Pallas kernels for 0%

commit v1 on v0

v1 whole, which is shorter than its diff:
```python
import functools
import math

import jax
import jax.numpy as jnp
from jax import lax
from jax.experimental import pallas as pl
from jax.experimental.pallas import tpu as pltpu
from jax.sharding import PartitionSpec as P

MESH = pl.DeviceIdType.MESH


def gelu_value(v):
    return 0.5 * v * (1.0 + lax.erf(v * (1.0 / math.sqrt(2.0))))


def gelu_slope(v):
    return 0.5 * (1.0 + lax.erf(v * (1.0 / math.sqrt(2.0)))) + v * jnp.exp(-0.5 * v * v) * (
        1.0 / math.sqrt(2.0 * math.pi)
    )


def shifted(x, axis, by):
    peers = lax.axis_size(axis)
    pairs = [(i, i + by) for i in range(peers) if 0 <= i + by < peers]
    return lax.ppermute(x, axis, pairs)


def place():
    s, f = lax.axis_index("seq"), lax.axis_index("fsdp")
    return s // 2, s % 2, f // 2, f % 2


def flip(x, y, c, first, second):
    fx = (1 - c) * first + c * second
    fy = c * first + (1 - c) * second
    return x + fx * (1 - 2 * x), y + fy * (1 - 2 * y)


def at(z, x, y, c):
    return (z * 2 + x, y * 2 + c)


def remote(src, dst, send, recv, device):
    return pltpu.make_async_remote_copy(
        src_ref=src, dst_ref=dst, send_sem=send, recv_sem=recv, device_id=device,
        device_id_type=MESH,
    )


def greet(n, z, x, y, c):
    barrier = pltpu.get_barrier_semaphore()
    peers = [at(z, 1 - x, y, c), at(z, x, 1 - y, c), at(z, x, y, 1 - c)]
    for peer in peers:
        pl.semaphore_signal(barrier, inc=1, device_id=peer, device_id_type=MESH)

    def hello(j, carry):
        pl.semaphore_signal(
            barrier, inc=1, device_id=at((z + j) % n, x, y, c), device_id_type=MESH
        )
        return carry

    lax.fori_loop(1, n, hello, 0)
    return barrier


def loop(lo, hi, f):
    def step(i, carry):
        f(i)
        return carry

    lax.fori_loop(lo, hi, step, 0)


def gather_kernel(n, shift, pack, acts, full, back, ahead, own_sem, zs, zr, as_, ar, bs, br, cs,
                  cr, hs, hr):
    z, x, y, c = place()
    linear = (z * 2 + x) * 4 + y * 2 + c
    total = n * 8
    barrier = greet(n, z, x, y, c)
    has_next = linear + shift < total
    has_prev = linear >= shift
    nxt = ((linear + shift) // 4, (linear + shift) % 4)
    prv = ((linear + total - shift) // 4 % (2 * n), (linear + total - shift) % 4)

    @pl.when(has_next)
    def _():
        pl.semaphore_signal(barrier, inc=1, device_id=nxt, device_id_type=MESH)

    @pl.when(has_prev)
    def _():
        pl.semaphore_signal(barrier, inc=1, device_id=prv, device_id_type=MESH)

    near = 2 - (linear + shift) // total - (total - 1 - linear + shift) // total
    pl.semaphore_wait(barrier, 3 + n - 1 + near)

    def spot(zz, xx, yy, cc):
        return full.at[yy * 2 + cc, zz * 2 + xx]

    x1, y1 = flip(x, y, c, 1, 0)
    x2, y2 = flip(x, y, c, 0, 1)
    to_a, to_b, to_c = at(z, x1, y1, c), at(z, x2, y2, c), at(z, x, y, 1 - c)
    own = spot(z, x, y, c)
    keep = pltpu.make_async_copy(pack, own, own_sem)
    keep.start()

    def send_z(j):
        remote(pack, own, zs.at[j], zr.at[j], at((z + j) % n, x, y, c)).start()

    def send_abc(j, src, dst):
        remote(src, dst, as_.at[j], ar.at[j], to_a).start()
        remote(src, dst, bs.at[j], br.at[j], to_b).start()
        remote(src, dst, cs.at[j], cr.at[j], to_c).start()

    loop(1, n, send_z)
    send_abc(0, pack, own)

    @pl.when(has_next)
    def _():
        remote(acts, back, hs.at[0], hr.at[0], nxt).start()

    @pl.when(has_prev)
    def _():
        remote(acts, ahead, hs.at[1], hr.at[1], prv).start()

    def zof(j):
        return (z + n - j) % n

    def step_z(j):
        b = spot(zof(j), x, y, c)
        remote(b, b, zs.at[j], zr.at[j], to_a).wait_recv()
        send_abc(j, b, b)

    loop(1, n, step_z)

    def step_a(j):
        b = spot(zof(j), x1, y1, c)
        remote(b, b, as_.at[j], ar.at[j], to_a).wait_recv()
        remote(b, b, bs.at[n + j], br.at[n + j], to_b).start()
        remote(b, b, cs.at[n + j], cr.at[n + j], to_c).start()

    loop(0, n, step_a)

    def step_b(m):
        fx, fy = flip(x, y, c, m // n, 1)
        b = spot(zof(m % n), fx, fy, c)
        remote(b, b, bs.at[m], br.at[m], to_b).wait_recv()
        remote(b, b, cs.at[2 * n + m], cr.at[2 * n + m], to_c).start()

    loop(0, 2 * n, step_b)

    def step_c(m):
        q = m // n
        fx, fy = flip(x, y, 1 - c, q % 2, q // 2)
        b = spot(zof(m % n), fx, fy, 1 - c)
        remote(b, b, cs.at[m], cr.at[m], to_c).wait_recv()

    loop(0, 4 * n, step_c)

    def sent(sems, recv):
        def f(j):
            remote(pack, own, sems.at[j], recv.at[j], to_a).wait_send()

        return f

    loop(1, n, sent(zs, zr))
    loop(0, n, sent(as_, ar))
    loop(0, 2 * n, sent(bs, br))
    loop(0, 4 * n, sent(cs, cr))
    keep.wait()

    @pl.when(has_next)
    def _():
        remote(acts, ahead, hs.at[0], hr.at[1], nxt).wait()

    @pl.when(has_prev)
    def _():
        remote(acts, back, hs.at[1], hr.at[0], prv).wait()


def reduce_kernel(n, norm, left, right, out, sa, ka, ra, rb, rc, rd, as_, ar, bs, br, cs, cr,
                  ds, dr):
    z, x, y, c = place()
    barrier = greet(n, z, x, y, c)
    x1, y1 = flip(x, y, c, 1, 0)
    x2, y2 = flip(x, y, c, 0, 1)
    to_c, to_b, to_a = at(z, x1, y1, c), at(z, x2, y2, c), at(z, x, y, 1 - c)

    def zof(t):
        return (z + t + 1) % n

    def block(m, core):
        q = m // n
        fx, fy = flip(x, y, core, 1 - q % 2, 1 - q // 2)
        s, f = at(zof(m % n), fx, fy, core)
        return jnp.dot(left[s], right[f], preferred_element_type=jnp.float32)

    sa[0] = block(0, 1 - c).astype(sa.dtype)
    pl.semaphore_wait(barrier, 3 + n - 1)

    def copy_a(m):
        return remote(sa.at[m], ra.at[m], as_.at[m], ar.at[m], to_a)

    def copy_b(m):
        return remote(ra.at[m], rb.at[m], bs.at[m], br.at[m], to_b)

    def copy_c(j):
        return remote(ra.at[2 * n + j], rc.at[j], cs.at[j], cr.at[j], to_c)

    def copy_d(t):
        return remote(ra.at[3 * n + t], rd.at[t], ds.at[t], dr.at[t], at(zof(t), x, y, c))

    copy_a(0).start()

    def step_send(m):
        sa[m] = block(m, 1 - c).astype(sa.dtype)
        copy_a(m).start()

    loop(1, 4 * n, step_send)

    def step_b(m):
        mine = block(m, c)
        copy_a(m).wait_recv()
        ra[m] = (ra[m].astype(jnp.float32) + mine).astype(ra.dtype)
        copy_b(m).start()

    loop(0, 2 * n, step_b)

    def step_k(m):
        ka[m] = block(2 * n + m, c).astype(ka.dtype)

    loop(0, 2 * n, step_k)

    def three(m):
        copy_a(2 * n + m).wait_recv()
        copy_b(m).wait_recv()
        return (
            ra[2 * n + m].astype(jnp.float32)
            + ka[m].astype(jnp.float32)
            + rb[m].astype(jnp.float32)
        )

    def step_c(j):
        ra[2 * n + j] = three(j).astype(ra.dtype)
        copy_c(j).start()

    loop(0, n, step_c)

    def step_d(t):
        part = three(n + t)
        copy_c(t).wait_recv()
        ra[3 * n + t] = (part + rc[t].astype(jnp.float32)).astype(ra.dtype)
        copy_d(t).start()

    loop(0, n - 1, step_d)
    part = three(2 * n - 1)
    copy_c(n - 1).wait_recv()
    out[...] = part + rc[n - 1].astype(jnp.float32)

    def step_out(t):
        copy_d(t).wait_recv()
        out[...] += rd[t].astype(jnp.float32)

    loop(0, n - 1, step_out)
    out[...] = out[...] * norm
    loop(0, 4 * n, lambda m: copy_a(m).wait_send())
    loop(0, 2 * n, lambda m: copy_b(m).wait_send())
    loop(0, n, lambda m: copy_c(m).wait_send())
    loop(0, n - 1, lambda m: copy_d(m).wait_send())


def body(inputs, cotangent, dilated_kernel_weight, point_weight):
    seqs, bins, width = inputs.shape
    peers, cols = lax.axis_size("seq"), lax.axis_size("fsdp")
    n = peers // 2
    shift = 128 // bins
    rows = seqs * bins
    norm_factor = 1.0 / math.sqrt(rows * peers * cols)
    wr, _, wc = dilated_kernel_weight.shape
    bf, f32 = jnp.bfloat16, jnp.float32
    pack = jnp.concatenate(
        [dilated_kernel_weight[:, 0], dilated_kernel_weight[:, 1], dilated_kernel_weight[:, 2],
         point_weight], axis=1)
    x = inputs.astype(f32).reshape(rows, width)
    cot = cotangent.reshape(rows, width)
    scale = lax.rsqrt(jnp.mean(x * x, axis=-1, keepdims=True) + 1e-06)
    normed = x * scale
    acts = gelu_value(normed).astype(bf)
    sem = pltpu.SemaphoreType.DMA
    anyspec = pl.BlockSpec(memory_space=pl.ANY)
    vspec = pl.BlockSpec(memory_space=pltpu.VMEM)
    full, back, ahead = pl.pallas_call(
        functools.partial(gather_kernel, n, shift),
        out_shape=(
            jax.ShapeDtypeStruct((cols, peers, wr, 4 * wc), bf),
            jax.ShapeDtypeStruct((rows, width), bf),
            jax.ShapeDtypeStruct((rows, width), bf),
        ),
        in_specs=[anyspec, anyspec],
        out_specs=[anyspec, anyspec, anyspec],
        scratch_shapes=[sem(()), sem((n,)), sem((n,)), sem((n,)), sem((n,)), sem((2 * n,)),
                        sem((2 * n,)), sem((4 * n,)), sem((4 * n,)), sem((2,)), sem((2,))],
        compiler_params=pltpu.CompilerParams(collective_id=0, has_side_effects=True),
    )(pack, acts)
    linear = lax.axis_index("seq") * cols + lax.axis_index("fsdp")
    back = jnp.where(linear >= shift, back, jnp.zeros((), bf))
    ahead = jnp.where(linear + shift < peers * cols, ahead, jnp.zeros((), bf))
    full = full.reshape(cols, width, 4 * wc)
    stacked = jnp.concatenate([back, acts, ahead, cot], axis=0)
    prod = [jnp.dot(stacked, full[f], preferred_element_type=f32) for f in range(cols)]
    hidden = jnp.stack([
        p[:rows, :wc] + p[rows:2 * rows, wc:2 * wc] + p[2 * rows:3 * rows, 2 * wc:3 * wc]
        for p in prod])
    back_mid = jnp.stack([p[3 * rows:, 3 * wc:] for p in prod])
    mid = gelu_value(hidden).astype(bf)
    grad = (back_mid * gelu_slope(hidden)).astype(bf)
    later = shifted(grad, ("seq", "fsdp"), -shift)
    earlier = shifted(grad, ("seq", "fsdp"), shift)
    none = jnp.zeros_like(grad)
    right = jnp.concatenate([
        jnp.concatenate([later, grad, earlier, none], axis=2),
        jnp.concatenate([none, none, none, mid], axis=2)], axis=1)
    left = jnp.concatenate([acts, cot], axis=0).T.reshape(peers, wr, 2 * rows)
    slot = lambda k: pltpu.VMEM((k, wr, 4 * wc), bf)
    reduced = pl.pallas_call(
        functools.partial(reduce_kernel, n, norm_factor),
        out_shape=jax.ShapeDtypeStruct((wr, 4 * wc), f32),
        in_specs=[vspec, vspec],
        out_specs=vspec,
        scratch_shapes=[slot(4 * n), slot(2 * n), slot(4 * n), slot(2 * n), slot(n), slot(n - 1),
                        sem((4 * n,)), sem((4 * n,)), sem((2 * n,)), sem((2 * n,)), sem((n,)),
                        sem((n,)), sem((n - 1,)), sem((n - 1,))],
        compiler_params=pltpu.CompilerParams(
            collective_id=1, has_side_effects=True, vmem_limit_bytes=52 * 1024 * 1024),
    )(left, right)
    both = sum(
        lax.dot_general(right[f], full[f], (((1,), (1,)), ((), ())), preferred_element_type=f32)
        for f in range(cols))
    outputs = (x + both[rows:]).astype(bf).reshape(seqs, bins, width)
    grad_normed = both[:rows] * gelu_slope(normed)
    inner = jnp.mean(grad_normed * x, axis=-1, keepdims=True)
    grad_inputs = (
        cot.astype(f32) + scale * (grad_normed - x * scale * scale * inner)
    ).astype(bf).reshape(seqs, bins, width)
    grad_conv = reduced[:, :3 * wc].reshape(wr, 3, wc)
    grad_point = reduced[:, 3 * wc:]
    return (outputs, grad_inputs, grad_conv, grad_point)


def solution(mesh):
    specs = (
        P(None, ("seq", "fsdp"), None),
        P(None, ("seq", "fsdp"), None),
        P("seq", None, "fsdp"),
        P("seq", "fsdp"),
    )
    return jax.shard_map(body, mesh=mesh, in_specs=specs, out_specs=specs, check_vma=False)
```

time: 597 us -> 220 us (0.37)
  waiting for transfers between devices: 477 us -> 17.2 us
  Pallas kernels: 0 us -> 141 us
  blocking collectives: 32.1 us -> 0 us
  local copies, waits for them, and re-layouts: 26.1 us -> 12.6 us
  between operations: 14 us -> 0.92 us
    reduce_scatter x1 -> x0, waiting for transfers between devices: 316 us -> none  [body(): lax.psum_scatter(jnp.concatenate([conv_part, point_part], axis=1).reshape...]
    pallas_call x0 -> x2, Pallas kernels: none -> 141 us  [the longest x1 77.7 us: body(): pl.pallas_call(functools.partial(gather_kernel, n, shift), out_shape=(jax...]
    all_gather x3 -> x0, waiting for transfers between devices: 125 us -> none  [the longest x1 64.7 us: body(): lax.all_gather(dilated_kernel_weight, 'seq', axis=0, tiled=True)]
    all_gather x1 -> x0, blocking collectives: 32.1 us -> none  [body(): lax.all_gather(point_weight, 'seq', axis=0, tiled=True)]
    unnamed x6 -> x0, waiting for transfers between devices: 21.1 us -> none
    unnamed x28 -> x31, local copies, waits for them, and re-layouts: 12.4 us -> 1.87 us
    slice x1 -> x5, local copies, waits for them, and re-layouts: 0.21 us -> 7.93 us  [the longest x1 6.85 us: body(): full[f]]
    reshape x1 -> x0, local copies, waits for them, and re-layouts: 6.99 us -> none  [body(): jnp.concatenate([conv_part, point_part], axis=1)]
  transfers between devices with their start and end apart: 9 -> 2, of which waited for: 6 -> 2; matrix products, arithmetic and copies ran while one was open for 3% -> 2% of each run, Pallas kernels for 0% -> 0%
where the time goes in v1:
time: 220 us; the launch traced here: 218 us
  Pallas kernels  141 us (64%)
  matrix products  22.3 us (10%)
  waiting for transfers between devices  17.2 us (8%)
  other arithmetic  14.4 us (7%)
  local copies, waits for them, and re-layouts  12.6 us (6%)
  starting transfers between devices  8.87 us (4%)
    pallas_call x1, Pallas kernels, body(): pl.pallas_call(functools.partial(gather_kernel, n, shift), out_shape=(jax...  77.7 us
    pallas_call x1, Pallas kernels, body(): pl.pallas_call(functools.partial(reduce_kernel, n, norm_factor), out_shap...  63.5 us
    ppermute x2, waiting for transfers between devices, shifted(): return lax.ppermute(x, axis, pairs)  17.2 us
    dot_general x4, matrix products, body(): jnp.dot(stacked, full[f], preferred_element_type=f32)  12.2 us
    dot_general x4, matrix products, body(): lax.dot_general(right[f], full[f], (((1,), (1,)), ((), ())), preferred_el...  10.1 us
    ppermute x2, starting transfers between devices, shifted(): return lax.ppermute(x, axis, pairs)  8.87 us
    slice x1, local copies, waits for them, and re-layouts, body(): full[f]  6.85 us
  transfers between devices with their start and end apart: 2, of which 2 were waited for; matrix products, arithmetic and copies ran while one was open for 2% of the time, Pallas kernels for 0%

profile of v1, /device:TPU:0, one launch (start us, length us, event | category | flops | bytes accessed | tf_op | source)
XLA Modules:
  0.0 217.5 jit_solution(11186317584450130361)
XLA Ops:
  0.7 1.4 fusion.20
  2.2 2.5 %fusion.12 = (bf16[256,1536]{1,0:T(8,128)(2,1)}, f32[256,1536]{1,0:T(8,128)S(1)}) fusion(bf16[4,64,1536]{2,1,0:T(8,128)(2,1)} %param.4, f32[256]{0:T(256)S(1)} %rsqrt.12), kind=kLoop, calls=%fused_computation.23 | loop fusion | flops 2752512 | bytes 3146752 | tf_op jit(solution)/shard_map/convert_element_type | solution.py:289
  5.5 77.7 %shard_map.75 = (bf16[4,8,192,768]{3,2,1,0:T(8,128)(2,1)}, bf16[256,1536]{1,0:T(8,128)(2,1)}, bf16[256,1536]{1,0:T(8,128)(2,1)}) custom-call(bf16[192,768]{1,0:T(8,128)(2,1)} %pad_maximum_fusion.2.pack, bf16[256,1536]{1,0:T(8,128)(2,1)} %get-tuple-element.18.acts), custom_call_target="tpu_custom_call" | custom-call | tf_op jit(solution)/shard_map/pallas_call | solution.py:293
  83.3 6.9 %fusion.38 = (bf16[1,8,192,768]{3,2,1,0:T(8,128)(2,1)}, bf16[1,8,192,768]{3,2,1,0:T(8,128)(2,1)}, bf16[1,8,192,768]{3,2,1,0:T(8,128)(2,1)}, bf16[1,8,192,768]{3,2,1,0:T(8,128)(2,1)}) fusion(bf16[4,8,192,768]{3,2,1,0:T(8,128)(2,1)} %get-tuple-element.9), kind=kLoop, calls=%fused_computation.76 | loop fusion | bytes 18874368 | tf_op jit(solution)/shard_map/slice | solution.py:311
  90.1 1.4 broadcast_select_fusion
  91.7 4.4 %fusion.36 = f32[1024,768]{1,0:T(8,128)S(1)} fusion(bf16[1536,768]{1,0:T(8,128)(2,1)} %bitcast.103, bf16[256,1536]{1,0:T(8,128)(2,1)S(1)} %bitcast.98, bf16[256,1536]{1,0:T(8,128)(2,1)S(1)} %get-tuple-element.39, bf16[256,1536]{1,0:T(8,128)(2,1)S(1)} %copy-done.9, bf16[256,1536]{1,0:T(8,128)(2,1)S(1)} %get-tuple-element.40), kind=kOutput, calls=%fused_computation.75 | convolution fusion | flops 2428502016 | bytes 8650752 | tf_op jit(solution)/shard_map/dot_general | solution.py:311
  96.4 2.6 %fusion.35 = f32[1024,768]{1,0:T(8,128)S(1)} fusion(bf16[1536,768]{1,0:T(8,128)(2,1)S(1)} %bitcast.96, bf16[256,1536]{1,0:T(8,128)(2,1)S(1)} %bitcast.99, bf16[256,1536]{1,0:T(8,128)(2,1)S(1)} %get-tuple-element.39, bf16[256,1536]{1,0:T(8,128)(2,1)S(1)} %copy-done.9, bf16[256,1536]{1,0:T(8,128)(2,1)S(1)} %get-tuple-element.40), kind=kOutput, calls=%fused_computation.74 | convolution fusion | flops 2428502016 | bytes 8650752 | tf_op jit(solution)/shard_map/dot_general | solution.py:311
  99.2 2.6 %fusion.34 = f32[1024,768]{1,0:T(8,128)S(1)} fusion(bf16[1536,768]{1,0:T(8,128)(2,1)S(1)} %bitcast.93, bf16[256,1536]{1,0:T(8,128)(2,1)S(1)} %bitcast.100, bf16[256,1536]{1,0:T(8,128)(2,1)S(1)} %get-tuple-element.39, bf16[256,1536]{1,0:T(8,128)(2,1)S(1)} %copy-done.9, bf16[256,1536]{1,0:T(8,128)(2,1)S(1)} %get-tuple-element.40), kind=kOutput, calls=%fused_computation.73 | convolution fusion | flops 2428502016 | bytes 8650752 | tf_op jit(solution)/shard_map/dot_general | solution.py:311
  102.0 2.6 %fusion.33 = f32[1024,768]{1,0:T(8,128)S(1)} fusion(bf16[1536,768]{1,0:T(8,128)(2,1)S(1)} %bitcast.91, bf16[256,1536]{1,0:T(8,128)(2,1)S(1)} %bitcast.101, bf16[256,1536]{1,0:T(8,128)(2,1)S(1)} %get-tuple-element.39, bf16[256,1536]{1,0:T(8,128)(2,1)S(1)} %copy-done.9, bf16[256,1536]{1,0:T(8,128)(2,1)S(1)} %get-tuple-element.40), kind=kOutput, calls=%fused_computation.72 | convolution fusion | flops 2428502016 | bytes 8650752 | tf_op jit(solution)/shard_map/dot_general | solution.py:311
  105.4 1.3 collective-permute-start
  106.7 7.6 %collective-permute-start.1 = (bf16[4,256,192]{2,1,0:T(8,128)(2,1)S(1)}, bf16[4,256,192]{2,1,0:T(8,128)(2,1)}, u32[]{:S(2)}, u32[]{:S(2)}) collective-permute-start(bf16[4,256,192]{2,1,0:T(8,128)(2,1)S(1)} %get-tuple-element.34), channel_id=1, source_target_pairs={{0,2},{1,3},{2,4},{3,5},{4,6},{5,7},{6,8},{7,9},{8,10},{9,11},{10,... | collective-permute-start | bytes 1179656 | tf_op jit(solution)/shard_map/ppermute | solution.py:27
  114.2 1.3 maximum_bitcast_fusion
  115.6 2.6 %copy.42 = bf16[1536,512]{1,0:T(8,128)(2,1)} copy(bf16[1536,512]{0,1:T(8,128)(2,1)} %maximum_bitcast_fusion) | data formatting | bytes 3145728 | tf_op jit(solution)/shard_map/transpose | solution.py:324
  118.3 5.9 %collective-permute-done = bf16[4,256,192]{2,1,0:T(8,128)(2,1)} collective-permute-done((bf16[4,256,192]{2,1,0:T(8,128)(2,1)S(1)}, bf16[4,256,192]{2,1,0:T(8,128)(2,1)}, u32[]{:S(2)}, u32[]{:S(2)}) %collective-permute-start) | collective-permute-done | bytes 393248 | tf_op jit(solution)/shard_map/ppermute | solution.py:27
  124.2 11.3 %collective-permute-done.1 = bf16[4,256,192]{2,1,0:T(8,128)(2,1)} collective-permute-done((bf16[4,256,192]{2,1,0:T(8,128)(2,1)S(1)}, bf16[4,256,192]{2,1,0:T(8,128)(2,1)}, u32[]{:S(2)}, u32[]{:S(2)}) %collective-permute-start.1) | collective-permute-done | bytes 393248 | tf_op jit(solution)/shard_map/ppermute | solution.py:27
  135.5 2.5 %fusion.1.right = bf16[4,512,768]{2,1,0:T(8,128)(2,1)S(1)} fusion(bf16[4,256,192]{2,1,0:T(8,128)(2,1)S(1)} %get-tuple-element.35, bf16[4,256,192]{2,1,0:T(8,128)(2,1)} %collective-permute-done.1, bf16[4,256,192]{2,1,0:T(8,128)(2,1)S(1)} %get-tuple-element.34, bf16[4,256,192]{2,1,0:T(8,128)(2,1)} %collective-permute-done, bf16[512,768]{1,0:T(8,128)(2,1)S(1)} %pad.6.clone), kind=kLoop, calls=%fused_computation.5 | loop fusion | flops 18874368 | bytes 5505024 | tf_op jit(solution)/shard_map/concatenate | solution.py:321
  138.0 3.1 %fusion.28 = f32[512,1536]{1,0:T(8,128)} fusion(bf16[1536,768]{1,0:T(8,128)(2,1)S(1)} %bitcast.104, bf16[4,512,768]{2,1,0:T(8,128)(2,1)S(1)} %fusion.1.right), kind=kOutput, calls=%fused_computation.47 | convolution fusion | flops 1207959552 | bytes 6291456 | tf_op jit(solution)/shard_map/dot_general | solution.py:338
  141.1 63.5 %shard_map.76 = f32[192,768]{1,0:T(8,128)S(1)} custom-call(bf16[8,192,512]{2,1,0:T(8,128)(2,1)} %bitcast.97, bf16[4,512,768]{2,1,0:T(8,128)(2,1)} %copy-done.1), custom_call_target="tpu_custom_call" | custom-call | tf_op jit(solution)/shard_map/pallas_call | solution.py:326
  204.6 0.9 slice.131
  205.5 4.2 %convolution_add_fusion.2 = f32[512,1536]{1,0:T(8,128)S(1)} fusion(f32[512,1536]{1,0:T(8,128)} %fusion.28, bf16[1536,768]{1,0:T(8,128)(2,1)} %bitcast.95, bf16[4,512,768]{2,1,0:T(8,128)(2,1)S(1)} %copy-done.2), kind=kOutput, calls=%fused_computation.4 | convolution fusion | flops 1208745984 | bytes 9437184 | tf_op jit(solution)/shard_map/dot_general | solution.py:338
  209.7 1.4 convolution_add_fusion.1
  211.3 1.4 convolution_add_fusion
  213.9 2.3 %fusion.19 = (bf16[256,1536]{1,0:T(8,128)(2,1)}, bf16[256,1536]{1,0:T(8,128)(2,1)}) fusion(bf16[4,64,1536]{2,1,0:T(8,128)(2,1)S(1)} %copy-done.3, f32[256]{0:T(256)S(1)} %broadcast_multiply_fusion, f32[256]{0:T(256)S(1)} %rsqrt.12, bf16[4,64,1536]{2,1,0:T(8,128)(2,1)S(1)} %copy-done.11, f32[256,1536]{1,0:T(8,128)S(1)} %get-tuple-element.19, ...), kind=kLoop, calls=%fused_computation.30 | loop fusion | flops 7077888 | bytes 7866368 | tf_op jit(solution)/shard_map/convert_element_type | solution.py:345
  216.4 1.1 copy.44
  (46 shorter events, 4.3 us)
Async XLA Ops:
  0.6 4.0 %copy-start.13 = (bf16[192,3,192]{2,0,1:T(8,128)(2,1)S(1)}, bf16[192,3,192]{2,0,1:T(8,128)(2,1)}, u32[]{:S(2)}) copy-start(bf16[192,3,192]{2,0,1:T(8,128)(2,1)} %param.6) | copy-start | bytes 663556
  0.6 4.0 %copy-start.14 = (bf16[192,192]{1,0:T(8,128)(2,1)S(1)}, bf16[192,192]{1,0:T(8,128)(2,1)}, u32[]{:S(2)}) copy-start(bf16[192,192]{1,0:T(8,128)(2,1)} %param.7) | copy-start | bytes 221188
  90.1 1.4 copy-start.9
  90.1 1.6 copy-start.10
  91.7 4.6 %copy-start.8 = (bf16[1,8,192,768]{3,2,1,0:T(8,128)(2,1)S(1)}, bf16[1,8,192,768]{3,2,1,0:T(8,128)(2,1)}, u32[]{:S(2)}) copy-start(bf16[1,8,192,768]{3,2,1,0:T(8,128)(2,1)} %get-tuple-element.20) | copy-start | bytes 7077892
  96.3 2.8 %copy-start.6 = (bf16[1,8,192,768]{3,2,1,0:T(8,128)(2,1)S(1)}, bf16[1,8,192,768]{3,2,1,0:T(8,128)(2,1)}, u32[]{:S(2)}) copy-start(bf16[1,8,192,768]{3,2,1,0:T(8,128)(2,1)} %get-tuple-element.22) | copy-start | bytes 7077892
  99.2 2.8 %copy-start.4 = (bf16[1,8,192,768]{3,2,1,0:T(8,128)(2,1)S(1)}, bf16[1,8,192,768]{3,2,1,0:T(8,128)(2,1)}, u32[]{:S(2)}) copy-start(bf16[1,8,192,768]{3,2,1,0:T(8,128)(2,1)} %get-tuple-element.21) | copy-start | bytes 7077892
  105.4 18.8 %collective-permute-start = (bf16[4,256,192]{2,1,0:T(8,128)(2,1)S(1)}, bf16[4,256,192]{2,1,0:T(8,128)(2,1)}, u32[]{:S(2)}, u32[]{:S(2)}) collective-permute-start(bf16[4,256,192]{2,1,0:T(8,128)(2,1)S(1)} %get-tuple-element.34), channel_id=1, source_target_pairs={{2,0},{3,1},{4,2},{5,3},{6,4},{7,5},{8,6},{9,7},{10,8},{11,9},{12,... | collective-permute-start | bytes 1179656 | tf_op jit(solution)/shard_map/ppermute | solution.py:27
  106.7 28.8 %collective-permute-start.1 = (bf16[4,256,192]{2,1,0:T(8,128)(2,1)S(1)}, bf16[4,256,192]{2,1,0:T(8,128)(2,1)}, u32[]{:S(2)}, u32[]{:S(2)}) collective-permute-start(bf16[4,256,192]{2,1,0:T(8,128)(2,1)S(1)} %get-tuple-element.34), channel_id=1, source_target_pairs={{0,2},{1,3},{2,4},{3,5},{4,6},{5,7},{6,8},{7,9},{8,10},{9,11},{10,... | collective-permute-start | bytes 1179656 | tf_op jit(solution)/shard_map/ppermute | solution.py:27
  118.3 19.7 %copy-start.12 = (bf16[1,8,192,768]{3,2,1,0:T(8,128)(2,1)S(1)}, bf16[1,8,192,768]{3,2,1,0:T(8,128)(2,1)}, u32[]{:S(2)}) copy-start(bf16[1,8,192,768]{3,2,1,0:T(8,128)(2,1)} %get-tuple-element.23) | copy-start | bytes 7077892
  138.0 3.1 %copy-start.1 = (bf16[4,512,768]{2,1,0:T(8,128)(2,1)}, bf16[4,512,768]{2,1,0:T(8,128)(2,1)S(1)}, u32[]{:S(2)}) copy-start(bf16[4,512,768]{2,1,0:T(8,128)(2,1)S(1)} %fusion.1.right) | copy-start | bytes 9437188
  141.1 64.4 %copy-start.2 = (bf16[4,512,768]{2,1,0:T(8,128)(2,1)S(1)}, bf16[4,512,768]{2,1,0:T(8,128)(2,1)}, u32[]{:S(2)}) copy-start(bf16[4,512,768]{2,1,0:T(8,128)(2,1)} %copy-done.1) | copy-start | bytes 9437188
  204.6 5.1 %copy-start = (f32[192,768]{1,0:T(8,128)}, f32[192,768]{1,0:T(8,128)S(1)}, u32[]{:S(2)}) copy-start(f32[192,768]{1,0:T(8,128)S(1)} %shard_map.76) | copy-start | bytes 1769476
  205.5 4.2 %copy-start.7 = (bf16[1,8,192,768]{3,2,1,0:T(8,128)(2,1)S(1)}, bf16[1,8,192,768]{3,2,1,0:T(8,128)(2,1)}, u32[]{:S(2)}) copy-start(bf16[1,8,192,768]{3,2,1,0:T(8,128)(2,1)} %get-tuple-element.22) | copy-start | bytes 7077892
  209.7 1.7 copy-start.5
  211.3 1.5 copy-start.3
  212.8 1.1 copy-start.11
  213.9 2.3 %slice-start = ((f32[192,768]{1,0:T(8,128)}), f32[192,576]{1,0:T(8,128)S(1)}, s32[]{:S(2)}) async-start(f32[192,768]{1,0:T(8,128)} %copy-done), calls=%async_computation | async-start | bytes 983040 | tf_op jit(solution)/shard_map/slice | solution.py:346

commit v2 on v0

v2 whole, which is shorter than its diff:
```python
import functools
import math

import jax
import jax.numpy as jnp
from jax import lax
from jax.experimental import pallas as pl
from jax.experimental.pallas import tpu as pltpu
from jax.sharding import PartitionSpec as P

MESH = pl.DeviceIdType.MESH


def gelu_value(v):
    return 0.5 * v * (1.0 + lax.erf(v * (1.0 / math.sqrt(2.0))))


def gelu_slope(v):
    return 0.5 * (1.0 + lax.erf(v * (1.0 / math.sqrt(2.0)))) + v * jnp.exp(-0.5 * v * v) * (
        1.0 / math.sqrt(2.0 * math.pi)
    )


def place():
    s, f = lax.axis_index("seq"), lax.axis_index("fsdp")
    return s // 2, s % 2, f // 2, f % 2


def flip(x, y, c, first, second):
    fx = (1 - c) * first + c * second
    fy = c * first + (1 - c) * second
    return x + fx * (1 - 2 * x), y + fy * (1 - 2 * y)


def at(z, x, y, c):
    return (z * 2 + x, y * 2 + c)


def remote(src, dst, send, recv, device):
    return pltpu.make_async_remote_copy(
        src_ref=src, dst_ref=dst, send_sem=send, recv_sem=recv, device_id=device,
        device_id_type=MESH,
    )


def greet(n, z, x, y, c):
    barrier = pltpu.get_barrier_semaphore()
    peers = [at(z, 1 - x, y, c), at(z, x, 1 - y, c), at(z, x, y, 1 - c)]
    for peer in peers:
        pl.semaphore_signal(barrier, inc=1, device_id=peer, device_id_type=MESH)

    def hello(j, carry):
        pl.semaphore_signal(
            barrier, inc=1, device_id=at((z + j) % n, x, y, c), device_id_type=MESH
        )
        return carry

    lax.fori_loop(1, n, hello, 0)
    return barrier


def loop(lo, hi, f):
    def step(i, carry):
        f(i)
        return carry

    lax.fori_loop(lo, hi, step, 0)


def line(n, shift, z, x, y, c):
    linear, total = (z * 2 + x) * 4 + y * 2 + c, n * 8
    has_next, has_prev = linear + shift < total, linear >= shift
    up, down = (linear + shift) % total, (linear + total - shift) % total
    near = 2 - (linear + shift) // total - (total - 1 - linear + shift) // total
    return has_next, has_prev, (up // 4, up % 4), (down // 4, down % 4), near


def greet_line(barrier, has_next, has_prev, nxt, prv):
    @pl.when(has_next)
    def _():
        pl.semaphore_signal(barrier, inc=1, device_id=nxt, device_id_type=MESH)

    @pl.when(has_prev)
    def _():
        pl.semaphore_signal(barrier, inc=1, device_id=prv, device_id_type=MESH)


def halo_start(has_next, has_prev, nxt, prv, up, down, from_prev, from_next, hs, hr):
    @pl.when(has_next)
    def _():
        remote(up, from_prev, hs.at[0], hr.at[0], nxt).start()

    @pl.when(has_prev)
    def _():
        remote(down, from_next, hs.at[1], hr.at[1], prv).start()


def halo_wait(has_next, has_prev, nxt, prv, up, down, from_prev, from_next, hs, hr):
    @pl.when(has_next)
    def _():
        remote(up, from_next, hs.at[0], hr.at[1], nxt).wait()

    @pl.when(has_prev)
    def _():
        remote(down, from_prev, hs.at[1], hr.at[0], prv).wait()

    @pl.when(jnp.logical_not(has_next))
    def _():
        from_next[...] = jnp.zeros_like(from_next)

    @pl.when(jnp.logical_not(has_prev))
    def _():
        from_prev[...] = jnp.zeros_like(from_prev)


def gather_kernel(n, shift, pack0, pack1, acts, full0, full1, back, ahead, up, down, own_sem, zs,
                  zr, as_, ar, bs, br, cs, cr, hs, hr):
    z, x, y, c = place()
    barrier = greet(n, z, x, y, c)
    has_next, has_prev, nxt, prv, near = line(n, shift, z, x, y, c)
    greet_line(barrier, has_next, has_prev, nxt, prv)
    pl.semaphore_wait(barrier, 3 + n - 1 + near)
    packs, fulls = (pack0, pack1), (full0, full1)

    def spot(h, zz, xx, yy, cc):
        return fulls[h].at[yy * 2 + cc, zz * 2 + xx]

    x1, y1 = flip(x, y, c, 1, 0)
    x2, y2 = flip(x, y, c, 0, 1)
    to_a, to_b, to_c = at(z, x1, y1, c), at(z, x2, y2, c), at(z, x, y, 1 - c)

    def zof(j):
        return (z + n - j) % n

    def copy_z(h, j):
        return remote(packs[h], spot(h, z, x, y, c), zs.at[h, j], zr.at[h, j],
                      at((z + j) % n, x, y, c))

    def copy_a(h, j, src, dst):
        return remote(src, dst, as_.at[h, j], ar.at[h, j], to_a)

    def copy_b(h, j, src, dst):
        return remote(src, dst, bs.at[h, j], br.at[h, j], to_b)

    def copy_c(h, j, src, dst):
        return remote(src, dst, cs.at[h, j], cr.at[h, j], to_c)

    def keep(h):
        return pltpu.make_async_copy(packs[h], spot(h, z, x, y, c), own_sem.at[h])

    def send_abc(h, j, src, dst):
        copy_a(h, j, src, dst).start()
        copy_b(h, j, src, dst).start()
        copy_c(h, j, src, dst).start()

    def own(h):
        loop(1, n, lambda j: copy_z(h, j).start())
        send_abc(h, 0, packs[h], spot(h, z, x, y, c))
        keep(h).start()

    def steps_z(h):
        def f(j):
            b = spot(h, zof(j), x, y, c)
            remote(b, b, zs.at[h, j], zr.at[h, j], to_a).wait_recv()
            send_abc(h, j, b, b)

        loop(1, n, f)

    def steps_a(h):
        def f(j):
            b = spot(h, zof(j), x1, y1, c)
            copy_a(h, j, b, b).wait_recv()
            copy_b(h, n + j, b, b).start()
            copy_c(h, n + j, b, b).start()

        loop(0, n, f)

    def steps_b(h):
        def f(m):
            fx, fy = flip(x, y, c, m // n, 1)
            b = spot(h, zof(m % n), fx, fy, c)
            copy_b(h, m, b, b).wait_recv()
            copy_c(h, 2 * n + m, b, b).start()

        loop(0, 2 * n, f)

    def steps_c(h):
        def f(m):
            q = m // n
            fx, fy = flip(x, y, 1 - c, q % 2, q // 2)
            b = spot(h, zof(m % n), fx, fy, 1 - c)
            copy_c(h, m, b, b).wait_recv()

        loop(0, 4 * n, f)

    def sent(h):
        b = spot(h, z, x, y, c)
        loop(1, n, lambda j: copy_z(h, j).wait_send())
        loop(0, n, lambda j: copy_a(h, j, b, b).wait_send())
        loop(0, 2 * n, lambda j: copy_b(h, j, b, b).wait_send())
        loop(0, 4 * n, lambda j: copy_c(h, j, b, b).wait_send())

    own(0)
    own(1)
    steps_z(0)
    steps_a(0)
    steps_b(0)
    steps_z(1)
    steps_c(0)
    keep(0).wait()
    rows, wc = acts.shape[1], pack0.shape[1] // 2
    parts = []
    for f in range(4):
        def add(s, total, f=f):
            return total + jnp.dot(acts[s], full0[f, s], preferred_element_type=jnp.float32)

        part = lax.fori_loop(0, 2 * n, add, jnp.zeros((rows, 2 * wc), jnp.float32))
        parts.append(part.astype(up.dtype))
    up[...] = jnp.concatenate([p[:, :wc] for p in parts], axis=1)
    down[...] = jnp.concatenate([p[:, wc:] for p in parts], axis=1)
    halo = (has_next, has_prev, nxt, prv, up, down, back, ahead, hs, hr)
    halo_start(*halo)
    steps_a(1)
    steps_b(1)
    steps_c(1)
    keep(1).wait()
    halo_wait(*halo)
    sent(0)
    sent(1)


def reduce_kernel(n, shift, norm, left, right, grad, out, edge, sa, ra, rb, rc, rd, later,
                  earlier, as_, ar, bs, br, cs, cr, ds, dr, hs, hr):
    z, x, y, c = place()
    barrier = greet(n, z, x, y, c)
    has_next, has_prev, nxt, prv, near = line(n, shift, z, x, y, c)
    greet_line(barrier, has_next, has_prev, nxt, prv)
    rows, wc2 = edge.shape[1:]
    wc = wc2 // 2
    x1, y1 = flip(x, y, c, 1, 0)
    x2, y2 = flip(x, y, c, 0, 1)
    to_c, to_b, to_a = at(z, x1, y1, c), at(z, x2, y2, c), at(z, x, y, 1 - c)

    def zof(t):
        return (z + t + 1) % n

    def block(h, m, core):
        q = m // n
        fx, fy = flip(x, y, core, 1 - q % 2, 1 - q // 2)
        s, f = at(zof(m % n), fx, fy, core)
        if h == 0:
            return jnp.dot(left[s], right[f], preferred_element_type=jnp.float32)
        return jnp.dot(left[s, :, :rows], edge[f], preferred_element_type=jnp.float32)

    sa[0, 0] = block(0, 0, 1 - c).astype(sa.dtype)
    pl.semaphore_wait(barrier, 3 + n - 1 + near)
    halo = (has_next, has_prev, nxt, prv, grad, grad, earlier, later, hs, hr)

    def copy_a(h, m):
        return remote(sa.at[h, m], ra.at[h, m], as_.at[h, m], ar.at[h, m], to_a)

    def copy_b(h, m):
        return remote(ra.at[h, m], rb.at[h, m], bs.at[h, m], br.at[h, m], to_b)

    def copy_c(h, j):
        return remote(ra.at[h, 2 * n + j], rc.at[h, j], cs.at[h, j], cr.at[h, j], to_c)

    def copy_d(h, t):
        return remote(ra.at[h, 3 * n + t], rd.at[h, t], ds.at[h, t], dr.at[h, t],
                      at(zof(t), x, y, c))

    def sends(h, first):
        def f(m):
            sa[h, m] = block(h, m, 1 - c).astype(sa.dtype)
            copy_a(h, m).start()

        loop(first, 4 * n, f)

    def steps_b(h):
        def f(m):
            mine = block(h, m, c)
            copy_a(h, m).wait_recv()
            ra[h, m] = (ra[h, m].astype(jnp.float32) + mine).astype(ra.dtype)
            copy_b(h, m).start()

        loop(0, 2 * n, f)

    def three(h, m):
        mine = block(h, 2 * n + m, c)
        copy_a(h, 2 * n + m).wait_recv()
        copy_b(h, m).wait_recv()
        return ra[h, 2 * n + m].astype(jnp.float32) + mine + rb[h, m].astype(jnp.float32)

    def steps_c(h):
        def f(j):
            ra[h, 2 * n + j] = three(h, j).astype(ra.dtype)
            copy_c(h, j).start()

        loop(0, n, f)

    def steps_d(h):
        def f(t):
            part = three(h, n + t)
            copy_c(h, t).wait_recv()
            ra[h, 3 * n + t] = (part + rc[h, t].astype(jnp.float32)).astype(ra.dtype)
            copy_d(h, t).start()

        loop(0, n - 1, f)
        part = three(h, 2 * n - 1)
        copy_c(h, n - 1).wait_recv()
        out[h] = part + rc[h, n - 1].astype(jnp.float32)

    def steps_out(h):
        def f(t):
            copy_d(h, t).wait_recv()
            out[h] += rd[h, t].astype(jnp.float32)

        loop(0, n - 1, f)
        out[h] = out[h] * norm

    copy_a(0, 0).start()
    halo_start(*halo)
    sends(0, 1)
    steps_b(0)
    halo_wait(*halo)
    for f in range(4):
        cols = slice(f * wc, (f + 1) * wc)
        edge[f] = jnp.concatenate([later[:, cols], earlier[:, cols]], axis=1)
    sends(1, 0)
    steps_b(1)
    steps_c(0)
    steps_c(1)
    steps_d(0)
    steps_d(1)
    steps_out(0)
    steps_out(1)
    for h in range(2):
        loop(0, 4 * n, lambda m: copy_a(h, m).wait_send())
        loop(0, 2 * n, lambda m: copy_b(h, m).wait_send())
        loop(0, n, lambda m: copy_c(h, m).wait_send())
        loop(0, n - 1, lambda m: copy_d(h, m).wait_send())


def body(inputs, cotangent, dilated_kernel_weight, point_weight):
    seqs, bins, width = inputs.shape
    peers, cols = lax.axis_size("seq"), lax.axis_size("fsdp")
    n = peers // 2
    shift = 128 // bins
    rows = seqs * bins
    norm_factor = 1.0 / math.sqrt(rows * peers * cols)
    wr, _, wc = dilated_kernel_weight.shape
    span = cols * wc
    bf, f32 = jnp.bfloat16, jnp.float32
    pack0 = jnp.concatenate([dilated_kernel_weight[:, 0], dilated_kernel_weight[:, 2]], axis=1)
    pack1 = jnp.concatenate([dilated_kernel_weight[:, 1], point_weight], axis=1)
    x = inputs.astype(f32).reshape(rows, width)
    cot = cotangent.reshape(rows, width)
    scale = lax.rsqrt(jnp.mean(x * x, axis=-1, keepdims=True) + 1e-06)
    normed = x * scale
    acts = gelu_value(normed).astype(bf)
    split = acts.reshape(rows, peers, wr).transpose(1, 0, 2)
    sem = lambda *k: pltpu.SemaphoreType.DMA(k)
    anyspec = pl.BlockSpec(memory_space=pl.ANY)
    vspec = pl.BlockSpec(memory_space=pltpu.VMEM)
    half = jax.ShapeDtypeStruct((cols, peers, wr, 2 * wc), bf)
    halo = jax.ShapeDtypeStruct((rows, span), bf)
    full0, full1, back, ahead = pl.pallas_call(
        functools.partial(gather_kernel, n, shift),
        out_shape=(half, half, halo, halo),
        in_specs=[anyspec, anyspec, vspec],
        out_specs=[vspec, anyspec, vspec, vspec],
        scratch_shapes=[pltpu.VMEM((rows, span), bf), pltpu.VMEM((rows, span), bf),
                        sem(2), sem(2, n), sem(2, n), sem(2, n), sem(2, n), sem(2, 2 * n),
                        sem(2, 2 * n), sem(2, 4 * n), sem(2, 4 * n), sem(2), sem(2)],
        compiler_params=pltpu.CompilerParams(
            collective_id=0, has_side_effects=True, vmem_limit_bytes=40 * 1024 * 1024),
    )(pack0, pack1, split)
    full0 = full0.reshape(cols, width, 2 * wc)
    full1 = full1.reshape(cols, width, 2 * wc)
    stacked = jnp.concatenate([acts, cot], axis=0)
    prod = [jnp.dot(stacked, full1[f], preferred_element_type=f32) for f in range(cols)]
    hidden = (jnp.concatenate([p[:rows, :wc] for p in prod], axis=1)
              + back.astype(f32) + ahead.astype(f32))
    back_mid = jnp.concatenate([p[rows:, wc:] for p in prod], axis=1)
    mid = gelu_value(hidden).astype(bf)
    grad = (back_mid * gelu_slope(hidden)).astype(bf)
    none = jnp.zeros((rows, wc), bf)
    right = jnp.stack([
        jnp.concatenate([
            jnp.concatenate([grad[:, f * wc:(f + 1) * wc], none], axis=1),
            jnp.concatenate([none, mid[:, f * wc:(f + 1) * wc]], axis=1)], axis=0)
        for f in range(cols)])
    left = stacked.T.reshape(peers, wr, 2 * rows)
    slot = lambda k: pltpu.VMEM((2, k, wr, 2 * wc), bf)
    reduced, edge = pl.pallas_call(
        functools.partial(reduce_kernel, n, shift, norm_factor),
        out_shape=(jax.ShapeDtypeStruct((2, wr, 2 * wc), f32),
                   jax.ShapeDtypeStruct((cols, rows, 2 * wc), bf)),
        in_specs=[vspec, vspec, vspec],
        out_specs=[vspec, vspec],
        scratch_shapes=[slot(4 * n), slot(4 * n), slot(2 * n), slot(n), slot(n - 1),
                        pltpu.VMEM((rows, span), bf), pltpu.VMEM((rows, span), bf),
                        sem(2, 4 * n), sem(2, 4 * n), sem(2, 2 * n), sem(2, 2 * n), sem(2, n),
                        sem(2, n), sem(2, n - 1), sem(2, n - 1), sem(2), sem(2)],
        compiler_params=pltpu.CompilerParams(
            collective_id=1, has_side_effects=True, vmem_limit_bytes=52 * 1024 * 1024),
    )(left, right, grad)
    against = (((1,), (1,)), ((), ()))
    both = sum(
        lax.dot_general(right[f], full1[f], against, preferred_element_type=f32)
        for f in range(cols))
    sides = sum(
        lax.dot_general(edge[f], full0[f], against, preferred_element_type=f32)
        for f in range(cols))
    outputs = (x + both[rows:]).astype(bf).reshape(seqs, bins, width)
    grad_normed = (both[:rows] + sides) * gelu_slope(normed)
    inner = jnp.mean(grad_normed * x, axis=-1, keepdims=True)
    grad_inputs = (
        cot.astype(f32) + scale * (grad_normed - x * scale * scale * inner)
    ).astype(bf).reshape(seqs, bins, width)
    grad_conv = jnp.stack([reduced[1, :, :wc], reduced[0, :, :wc], reduced[1, :, wc:]], axis=1)
    grad_point = reduced[0, :, wc:]
    return (outputs, grad_inputs, grad_conv, grad_point)


def solution(mesh):
    specs = (
        P(None, ("seq", "fsdp"), None),
        P(None, ("seq", "fsdp"), None),
        P("seq", None, "fsdp"),
        P("seq", "fsdp"),
    )
    return jax.shard_map(body, mesh=mesh, in_specs=specs, out_specs=specs, check_vma=False)
```

time: 597 us -> 186 us (0.31)
  the two profiles are of different devices: /device:TPU:0 before, /device:TPU:31 now
where the time goes in v2:
time: 186 us
  Pallas kernels  153 us (82%)
  local copies, waits for them, and re-layouts  11.3 us (6%)
  matrix products  10.9 us (6%)
  other arithmetic  9.64 us (5%)
    pallas_call x1, Pallas kernels, body(): pl.pallas_call(functools.partial(reduce_kernel, n, shift, norm_factor), o...  84.2 us
    pallas_call x1, Pallas kernels, body(): pl.pallas_call(functools.partial(gather_kernel, n, shift), out_shape=(hal...  68.8 us
    unnamed x64, local copies, waits for them, and re-layouts  5.22 us
    dot_general x4, matrix products, body(): lax.dot_general(right[f], full1[f], against, preferred_element_type=f32)  4.08 us
    dot_general x4, matrix products, body(): jnp.dot(stacked, full1[f], preferred_element_type=f32)  3.9 us

profile of v2, /device:TPU:31, one launch (start us, length us, event | category | flops | bytes accessed | tf_op | source)
XLA Modules:
  0.0 185.9 jit_solution(11014246155792535413)
XLA Ops:
  0.6 1.1 slice_bitcast_fusion.4
  1.7 1.0 pad_maximum_fusion.3
  3.1 0.7 reshape.73
  3.8 1.0 fusion.8.acts
  4.8 68.8 %shard_map.75 = (bf16[4,8,192,384]{3,2,1,0:T(8,128)(2,1)S(1)}, bf16[4,8,192,384]{3,2,1,0:T(8,128)(2,1)S(1)}, bf16[256,768]{1,0:T(8,128)(2,1)S(1)}, bf16[256,768]{1,0:T(8,128)(2,1)S(1)}) custom-call(bf16[192,384]{1,0:T(8,128)(2,1)S(1)} %get-tuple-element.55.pack0, bf16[192,384]{1,0:T(8,128)(2,1)S(1)} %get-tuple-element.56.pack1, ...), custom_call_target="tpu_custom_call" | custom-call | tf_op jit(solution)/shard_map/pallas_call | solution.py:367
  74.2 1.6 copy-done
  75.8 2.2 %multiply_convert_fusion.1 = (bf16[256,1536]{1,0:T(8,128)(2,1)S(1)}, f32[256,1536]{1,0:T(8,128)}, f32[256,1536]{1,0:T(8,128)}) fusion(bf16[4,64,1536]{2,1,0:T(8,128)(2,1)S(1)} %copy-done.1, f32[256]{0:T(256)S(1)} %rsqrt.12), kind=kLoop, calls=%fused_computation.23 | loop fusion | flops 2752512 | bytes 4719616 | tf_op jit(solution)/shard_map/convert_element_type | solution.py:360
  78.0 1.0 fusion.61
  79.1 1.0 fusion.60
  80.2 1.0 fusion.59
  81.3 1.0 fusion.58
  82.5 0.6 fusion.14
  85.0 1.4 pad_maximum_fusion.1.right
  86.5 1.6 copy.37
  88.1 84.2 %shard_map.76 = (f32[2,192,384]{2,1,0:T(8,128)S(1)}, bf16[4,256,384]{2,1,0:T(8,128)(2,1)S(1)}) custom-call(bf16[8,192,512]{2,1,0:T(8,128)(2,1)} %bitcast.80, bf16[4,512,384]{2,1,0:T(8,128)(2,1)} %pad_maximum_fusion.1.right, bf16[256,768]{1,0:T(8,128)(2,1)S(1)} %get-tuple-element.26.grad), custom_call_target="tpu_custom_call" | custom-call | tf_op jit(solution)/shard_map/pallas_call | solution.py:395
  172.3 0.8 slice_bitcast_fusion
  173.1 0.9 pad_maximum_fusion.2
  174.0 1.0 fusion.37
  175.3 1.0 convolution_add_fusion.2
  176.6 1.0 convolution_add_fusion.1
  177.9 1.0 convolution_add_fusion
  181.9 0.8 copy-done.2
  183.1 1.1 fusion.7
  184.2 1.7 add_convert_fusion
  (84 shorter events, 7.4 us)
Async XLA Ops:
  0.6 2.1 %copy-start.1 = (bf16[4,64,1536]{2,1,0:T(8,128)(2,1)S(1)}, bf16[4,64,1536]{2,1,0:T(8,128)(2,1)}, u32[]{:S(2)}) copy-start(bf16[4,64,1536]{2,1,0:T(8,128)(2,1)} %param.4) | copy-start | bytes 2359300
  73.6 2.1 %copy-start = (bf16[4,8,192,384]{3,2,1,0:T(8,128)(2,1)}, bf16[4,8,192,384]{3,2,1,0:T(8,128)(2,1)S(1)}, u32[]{:S(2)}) copy-start(bf16[4,8,192,384]{3,2,1,0:T(8,128)(2,1)S(1)} %get-tuple-element.14) | copy-start | bytes 14155780
  75.7 2.2 %copy-start.4 = (bf16[1,8,192,384]{3,2,1,0:T(8,128)(2,1)}, bf16[1,8,192,384]{3,2,1,0:T(8,128)(2,1)S(1)}, u32[]{:S(2)}) copy-start(bf16[1,8,192,384]{3,2,1,0:T(8,128)(2,1)S(1)} %get-tuple-element.25) | copy-start | bytes 3538948
  75.7 3.3 %copy-start.10 = (bf16[1,8,192,384]{3,2,1,0:T(8,128)(2,1)}, bf16[1,8,192,384]{3,2,1,0:T(8,128)(2,1)S(1)}, u32[]{:S(2)}) copy-start(bf16[1,8,192,384]{3,2,1,0:T(8,128)(2,1)S(1)} %get-tuple-element.22) | copy-start | bytes 3538948
  75.7 4.5 %copy-start.8 = (bf16[1,8,192,384]{3,2,1,0:T(8,128)(2,1)}, bf16[1,8,192,384]{3,2,1,0:T(8,128)(2,1)S(1)}, u32[]{:S(2)}) copy-start(bf16[1,8,192,384]{3,2,1,0:T(8,128)(2,1)S(1)} %get-tuple-element.24) | copy-start | bytes 3538948
  75.7 5.6 %copy-start.6 = (bf16[1,8,192,384]{3,2,1,0:T(8,128)(2,1)}, bf16[1,8,192,384]{3,2,1,0:T(8,128)(2,1)S(1)}, u32[]{:S(2)}) copy-start(bf16[1,8,192,384]{3,2,1,0:T(8,128)(2,1)S(1)} %get-tuple-element.23) | copy-start | bytes 3538948
  75.8 2.2 %copy-start.12 = (bf16[4,64,1536]{2,1,0:T(8,128)(2,1)S(1)}, bf16[4,64,1536]{2,1,0:T(8,128)(2,1)}, u32[]{:S(2)}) copy-start(bf16[4,64,1536]{2,1,0:T(8,128)(2,1)} %param.5) | copy-start | bytes 2359300
  83.3 1.6 copy-start.23
  83.3 1.6 copy-start.25
  83.3 1.6 copy-start.21
  83.3 1.6 copy-start.13
  172.3 1.7 copy-start.5
  172.3 1.7 copy-start.14
  172.3 1.7 copy-start.28
  174.0 1.3 copy-start.11
  174.0 1.3 copy-start.26
  175.3 1.3 copy-start.18
  175.3 1.3 copy-start.24
  176.6 1.3 copy-start.16
  176.6 1.3 copy-start.22
  176.6 2.6 %slice-start = ((s8[4718592]{0:T(1024)(128)(4,1)}), s8[4194304]{0:T(1024)(128)(4,1)S(1)}, s32[]{:S(2)}) async-start(s8[4718592]{0:T(1024)(128)(4,1)} %bitcast.78), calls=%async_computation | async-start | bytes 8388608
  177.9 1.6 slice-start.1
  181.2 1.4 copy-start.2
  181.2 1.9 %copy-start.3 = (f32[256,1536]{1,0:T(8,128)S(1)}, f32[256,1536]{1,0:T(8,128)}, u32[]{:S(2)}) copy-start(f32[256,1536]{1,0:T(8,128)} %get-tuple-element.28) | copy-start | bytes 4718596
  (8 other events, 7.6 us)

commit v3 on v2

--- a/solution.py
+++ b/solution.py
@@ -204,8 +204,9 @@
     own(1)
     steps_z(0)
     steps_a(0)
+    steps_z(1)
     steps_b(0)
-    steps_z(1)
+    steps_a(1)
     steps_c(0)
     keep(0).wait()
     rows, wc = acts.shape[1], pack0.shape[1] // 2
@@ -220,7 +221,6 @@
     down[...] = jnp.concatenate([p[:, wc:] for p in parts], axis=1)
     halo = (has_next, has_prev, nxt, prv, up, down, back, ahead, hs, hr)
     halo_start(*halo)
-    steps_a(1)
     steps_b(1)
     steps_c(1)
     keep(1).wait()
@@ -229,8 +229,8 @@
     sent(1)
 
 
-def reduce_kernel(n, shift, norm, left, right, grad, out, edge, sa, ra, rb, rc, rd, later,
-                  earlier, as_, ar, bs, br, cs, cr, ds, dr, hs, hr):
+def reduce_kernel(n, shift, norm, left, right, grad, whole0, whole1, out, both, edge, g0, g1, sa, ra,
+                  rb, rc, rd, later, earlier, gs, as_, ar, bs, br, cs, cr, ds, dr, hs, hr):
     z, x, y, c = place()
     barrier = greet(n, z, x, y, c)
     has_next, has_prev, nxt, prv, near = line(n, shift, z, x, y, c)
@@ -252,6 +252,10 @@
             return jnp.dot(left[s], right[f], preferred_element_type=jnp.float32)
         return jnp.dot(left[s, :, :rows], edge[f], preferred_element_type=jnp.float32)
 
+    load0 = pltpu.make_async_copy(whole0, g0, gs.at[0])
+    load1 = pltpu.make_async_copy(whole1, g1, gs.at[1])
+    load0.start()
+    load1.start()
     sa[0, 0] = block(0, 0, 1 - c).astype(sa.dtype)
     pl.semaphore_wait(barrier, 3 + n - 1 + near)
     halo = (has_next, has_prev, nxt, prv, grad, grad, earlier, later, hs, hr)
@@ -327,11 +331,29 @@
         cols = slice(f * wc, (f + 1) * wc)
         edge[f] = jnp.concatenate([later[:, cols], earlier[:, cols]], axis=1)
     sends(1, 0)
+    steps_c(0)
     steps_b(1)
-    steps_c(0)
+    steps_d(0)
     steps_c(1)
-    steps_d(0)
     steps_d(1)
+    load0.wait()
+    load1.wait()
+    tile = 256
+    against = (((1,), (1,)), ((), ()))
+
+    def product(t):
+        where = pl.ds(pl.multiple_of(t * tile, tile), tile)
+        total = jnp.zeros((2 * rows, tile), jnp.float32)
+        sides = jnp.zeros((rows, tile), jnp.float32)
+        for f in range(4):
+            total += lax.dot_general(right[f], g1[f, where, :], against,
+                                     preferred_element_type=jnp.float32)
+            sides += lax.dot_general(edge[f], g0[f, where, :], against,
+                                     preferred_element_type=jnp.float32)
+        both[:rows, where] = total[:rows] + sides
+        both[rows:, where] = total[rows:]
+
+    loop(0, both.shape[1] // tile, product)
     steps_out(0)
     steps_out(1)
     for h in range(2):
@@ -392,28 +414,22 @@
         for f in range(cols)])
     left = stacked.T.reshape(peers, wr, 2 * rows)
     slot = lambda k: pltpu.VMEM((2, k, wr, 2 * wc), bf)
-    reduced, edge = pl.pallas_call(
+    reduced, both = pl.pallas_call(
         functools.partial(reduce_kernel, n, shift, norm_factor),
         out_shape=(jax.ShapeDtypeStruct((2, wr, 2 * wc), f32),
-                   jax.ShapeDtypeStruct((cols, rows, 2 * wc), bf)),
-        in_specs=[vspec, vspec, vspec],
+                   jax.ShapeDtypeStruct((2 * rows, width), f32)),
+        in_specs=[vspec, vspec, vspec, anyspec, anyspec],
         out_specs=[vspec, vspec],
-        scratch_shapes=[slot(4 * n), slot(4 * n), slot(2 * n), slot(n), slot(n - 1),
+        scratch_shapes=[pltpu.VMEM((cols, rows, 2 * wc), bf), pltpu.VMEM(full0.shape, bf),
+                        pltpu.VMEM(full1.shape, bf), slot(4 * n), slot(4 * n), slot(2 * n), slot(n), slot(n - 1),
                         pltpu.VMEM((rows, span), bf), pltpu.VMEM((rows, span), bf),
-                        sem(2, 4 * n), sem(2, 4 * n), sem(2, 2 * n), sem(2, 2 * n), sem(2, n),
+                        sem(2), sem(2, 4 * n), sem(2, 4 * n), sem(2, 2 * n), sem(2, 2 * n), sem(2, n),
                         sem(2, n), sem(2, n - 1), sem(2, n - 1), sem(2), sem(2)],
         compiler_params=pltpu.CompilerParams(
             collective_id=1, has_side_effects=True, vmem_limit_bytes=52 * 1024 * 1024),
-    )(left, right, grad)
-    against = (((1,), (1,)), ((), ()))
-    both = sum(
-        lax.dot_general(right[f], full1[f], against, preferred_element_type=f32)
-        for f in range(cols))
-    sides = sum(
-        lax.dot_general(edge[f], full0[f], against, preferred_element_type=f32)
-        for f in range(cols))
+    )(left, right, grad, full0, full1)
     outputs = (x + both[rows:]).astype(bf).reshape(seqs, bins, width)
-    grad_normed = (both[:rows] + sides) * gelu_slope(normed)
+    grad_normed = both[:rows] * gelu_slope(normed)
     inner = jnp.mean(grad_normed * x, axis=-1, keepdims=True)
     grad_inputs = (
         cot.astype(f32) + scale * (grad_normed - x * scale * scale * inner)

time: 186 us -> 166 us (0.89)
  the two profiles are of different devices: /device:TPU:31 before, /device:TPU:0 now
where the time goes in v3:
time: 166 us; the launch traced here: 165 us
  Pallas kernels  138 us (83%)
  other arithmetic  12 us (7%)
  local copies, waits for them, and re-layouts  10.3 us (6%)
  matrix products  3.92 us (2%)
    pallas_call x1, Pallas kernels, body(): pl.pallas_call(functools.partial(reduce_kernel, n, shift, norm_factor), o...  73.5 us
    pallas_call x1, Pallas kernels, body(): pl.pallas_call(functools.partial(gather_kernel, n, shift), out_shape=(hal...  64.2 us
    dot_general x4, matrix products, body(): jnp.dot(stacked, full1[f], preferred_element_type=f32)  3.92 us
    unnamed x12, local copies, waits for them, and re-layouts  3.75 us

profile of v3, /device:TPU:0, one launch (start us, length us, event | category | flops | bytes accessed | tf_op | source)
XLA Modules:
  0.0 164.8 jit_solution(5484149263876136790)
XLA Ops:
  0.6 1.1 slice_bitcast_fusion.4
  1.7 1.0 pad_maximum_fusion.3
  2.8 0.2 multiply_reduce_fusion
  3.1 0.7 reshape.70
  3.8 1.0 fusion.7.acts
  4.8 64.2 %shard_map.75 = (bf16[4,8,192,384]{3,2,1,0:T(8,128)(2,1)S(1)}, bf16[4,8,192,384]{3,2,1,0:T(8,128)(2,1)S(1)}, bf16[256,768]{1,0:T(8,128)(2,1)S(1)}, bf16[256,768]{1,0:T(8,128)(2,1)S(1)}) custom-call(bf16[192,384]{1,0:T(8,128)(2,1)S(1)} %get-tuple-element.48.pack0, bf16[192,384]{1,0:T(8,128)(2,1)S(1)} %get-tuple-element.49.pack1, ...), custom_call_target="tpu_custom_call" | custom-call | tf_op jit(solution)/shard_map/pallas_call | solution.py:389
  69.1 0.5 fusion.35
  69.6 1.6 %copy-done = bf16[4,8,192,384]{3,2,1,0:T(8,128)(2,1)} copy-done((bf16[4,8,192,384]{3,2,1,0:T(8,128)(2,1)}, bf16[4,8,192,384]{3,2,1,0:T(8,128)(2,1)S(1)}, u32[]{:S(2)}) %copy-start) | copy-done | bytes 4718616
  71.2 1.4 copy-done.1
  72.6 0.4 multiply_convert_fusion.1
  73.1 0.7 copy-done.4
  73.8 1.0 fusion.33
  74.9 1.0 fusion.32
  76.0 1.0 fusion.31
  77.1 1.0 fusion.30
  78.2 0.7 fusion.13
  79.7 1.4 pad_maximum_fusion.1.right
  81.1 1.2 fusion.34
  82.3 2.6 %copy.27 = bf16[1536,512]{1,0:T(8,128)(2,1)} copy(bf16[1536,512]{0,1:T(8,128)(2,1)} %fusion.34) | data formatting | bytes 3145728 | tf_op jit(solution)/shard_map/transpose | solution.py:415
  85.0 73.5 %shard_map.76 = (f32[2,192,384]{2,1,0:T(8,128)S(1)}, f32[512,1536]{1,0:T(8,128)}) custom-call(bf16[8,192,512]{2,1,0:T(8,128)(2,1)} %bitcast.64, bf16[4,512,384]{2,1,0:T(8,128)(2,1)} %pad_maximum_fusion.1.right, bf16[256,768]{1,0:T(8,128)(2,1)S(1)} %get-tuple-element.24.grad, bf16[4,1536,384]{2,1,0:T(8,128)(2,1)} %bitcast.63, bf16[4,1536,384]{2,1,0:T(8,128)(2,1)} %bitcast.62), custom_call_target="tpu_custom_call" | custom-call | tf_op jit(solution)/shard_map/pallas_call | solution.py:417
  158.4 0.8 slice_bitcast_fusion
  159.3 0.9 pad_maximum_fusion.2
  160.1 2.4 %fusion.6 = f32[256]{0:T(256)S(1)} fusion(bf16[4,64,1536]{2,1,0:T(8,128)(2,1)S(1)} %copy-done.2, f32[256]{0:T(256)S(1)} %rsqrt.12, f32[256,1536]{1,0:T(8,128)S(1)} %get-tuple-element.17, f32[512,1536]{1,0:T(8,128)} %get-tuple-element.14), kind=kLoop, calls=%fused_computation.14 | loop fusion | flops 4325120 | bytes 3934208 | tf_op jit(solution)/shard_map/reduce_sum | solution.py:433
  162.5 2.3 %add_convert_fusion = (bf16[256,1536]{1,0:T(8,128)(2,1)}, bf16[256,1536]{1,0:T(8,128)(2,1)}) fusion(bf16[4,64,1536]{2,1,0:T(8,128)(2,1)S(1)} %copy-done.2, f32[256]{0:T(256)S(1)} %broadcast_multiply_fusion, f32[256]{0:T(256)S(1)} %rsqrt.12, bf16[4,64,1536]{2,1,0:T(8,128)(2,1)S(1)} %copy-done.4, f32[256,1536]{1,0:T(8,128)S(1)} %get-tuple-element.17, ...), kind=kLoop, calls=%fused_computation.15 | loop fusion | flops 7077888 | bytes 7866368 | tf_op jit(solution)/shard_map/convert_element_type | solution.py:436
  (23 shorter events, 1.4 us)
Async XLA Ops:
  0.6 2.1 %copy-start.2 = (bf16[4,64,1536]{2,1,0:T(8,128)(2,1)S(1)}, bf16[4,64,1536]{2,1,0:T(8,128)(2,1)}, u32[]{:S(2)}) copy-start(bf16[4,64,1536]{2,1,0:T(8,128)(2,1)} %param.4) | copy-start | bytes 2359300
  69.0 2.2 %copy-start = (bf16[4,8,192,384]{3,2,1,0:T(8,128)(2,1)}, bf16[4,8,192,384]{3,2,1,0:T(8,128)(2,1)S(1)}, u32[]{:S(2)}) copy-start(bf16[4,8,192,384]{3,2,1,0:T(8,128)(2,1)S(1)} %get-tuple-element.10) | copy-start | bytes 14155780
  69.0 3.6 %copy-start.1 = (bf16[4,8,192,384]{3,2,1,0:T(8,128)(2,1)}, bf16[4,8,192,384]{3,2,1,0:T(8,128)(2,1)S(1)}, u32[]{:S(2)}) copy-start(bf16[4,8,192,384]{3,2,1,0:T(8,128)(2,1)S(1)} %get-tuple-element.13) | copy-start | bytes 14155780
  72.6 1.1 copy-start.4
  78.2 0.8 copy-start.5
  160.1 2.4 %copy-start.3 = (f32[512,1536]{1,0:T(8,128)S(1)}, f32[512,1536]{1,0:T(8,128)}, u32[]{:S(2)}) copy-start(f32[512,1536]{1,0:T(8,128)} %get-tuple-element.14) | copy-start | bytes 9437188
